TPU v7x, 128 devices: a whole 4x4x4 slice. The times are simulated.
128 devices in a mesh: depth: 4 (over x), row: 16 (over z, y), col: 2 (over core).
Axes of the slice: x: 4, y: 4, z: 4, core: 2. Of those that a mesh axis runs over, the one named last changes fastest.
Arguments:
- acts: bfloat16 [1024, 6144], P(('depth', 'col'), 'row'), may hold values from -6 to 6
- cotangent: bfloat16 [1024, 6144], P(('depth', 'col'), 'row'), may hold values from -6 to 6
- pre_act: bfloat16 [1024, 12288], P(('depth', 'row'), 'col'), may hold values from -8 to 8
- w_in: bfloat16 [6144, 12288], P('row', 'col'), may hold values from -0.078125 to 0.078125
- w_out: bfloat16 [12288, 6144], P('col', 'row'), may hold values from -0.0546875 to 0.0546875
Outputs:
- grad_in: float32 [1024, 6144], P(('depth', 'col'), 'row')
- grad_w_in: float32 [16, 4, 96, 12288], P('row', 'depth', None, 'col')
- grad_w_out: float32 [2, 4, 1536, 6144], P('col', 'depth', None, 'row')
All inputs are finite; a program needn't handle non-finite values.
Results may differ from a plain program's by a relative error of at most 0.0029.
Values may be sent and summed in bfloat16 or wider, within the bound.
A program may use at most 128 MiB of HBM per device.

v0:
```python
import math

import jax
import jax.numpy as jnp
from jax import lax
from jax.sharding import PartitionSpec as P

SLICE_TOK = 256


gelu_coef = 0.044715


def gelu_value(v):
    inner = math.sqrt(2.0 / math.pi) * (v + gelu_coef * v * v * v)
    return 0.5 * v * (1.0 + jnp.tanh(inner))


def gelu_slope(v):
    inner = math.sqrt(2.0 / math.pi) * (v + gelu_coef * v * v * v)
    tanh_u = jnp.tanh(inner)
    return 0.5 * (1.0 + tanh_u) + 0.5 * v * (1.0 - tanh_u * tanh_u) * math.sqrt(2.0 / math.pi) * (
        1.0 + 3.0 * gelu_coef * v * v
    )


def times_transposed(left, right):
    return lax.dot_general(
        left, right, (((1,), (1,)), ((), ())), preferred_element_type=jnp.float32
    )


def transposed_times(left, right):
    return lax.dot_general(
        left, right, (((0,), (0,)), ((), ())), preferred_element_type=jnp.float32
    )


def on_device(acts, cotangent, pre_act, w_in, w_out):
    acts_all, cot_all = (
        lax.all_gather(acts, "col", axis=0, tiled=True),
        lax.all_gather(cotangent, "col", axis=0, tiled=True),
    )
    pre_all = lax.all_gather(pre_act, "row", axis=0, tiled=True).astype(jnp.float32)
    partial_act = times_transposed(cot_all, w_out)
    grad_act = lax.psum(partial_act, "row")
    grad_pre_all = (grad_act * gelu_slope(pre_all)).astype(jnp.bfloat16)
    hidden_all = gelu_value(pre_all).astype(jnp.bfloat16)
    grad_in = lax.psum_scatter(
        times_transposed(grad_pre_all, w_in), "col", scatter_dimension=0, tiled=True
    )
    norm_factor = 1.0 / math.sqrt(SLICE_TOK * lax.axis_size("depth"))
    in_rows = w_in.shape[0] // lax.axis_size("depth")
    out_rows = w_out.shape[0] // lax.axis_size("depth")
    grad_w_in = lax.psum_scatter(
        transposed_times(acts_all, grad_pre_all) * norm_factor,
        "depth",
        scatter_dimension=0,
        tiled=True,
    )
    grad_w_out = lax.psum_scatter(
        transposed_times(hidden_all, cot_all) * norm_factor,
        "depth",
        scatter_dimension=0,
        tiled=True,
    )
    grad_w_in = grad_w_in.reshape(1, 1, in_rows, w_in.shape[1])
    grad_w_out = grad_w_out.reshape(1, 1, out_rows, w_out.shape[1])
    return (grad_in, grad_w_in, grad_w_out)


def solution(mesh):
    in_specs = (
        P(("depth", "col"), "row"),
        P(("depth", "col"), "row"),
        P(("depth", "row"), "col"),
        P("row", "col"),
        P("col", "row"),
    )
    out_specs = (
        P(("depth", "col"), "row"),
        P("row", "depth", None, "col"),
        P("col", "depth", None, "row"),
    )
    return jax.shard_map(
        on_device, mesh=mesh, in_specs=in_specs, out_specs=out_specs, check_vma=False
    )
```

profile of v0, /device:TPU:0, one launch (start us, length us, event | category | flops | bytes accessed | tf_op | source)
XLA Modules:
  0.0 408.7 jit_solution(3036424780198616031)
XLA Ops:
  7.2 0.0 all-gather.2.cloned.1.call-start
  7.2 0.7 all-gather.2.cloned.1.call-update
  7.9 0.0 all-reduce.2.cloned.1.call-start
  7.9 2.2 all_gather.9
  10.1 0.0 copy-start
  10.1 6.8 %fusion.20 = f32[256,6144]{1,0:T(8,128)} fusion(bf16[256,384]{1,0:T(8,128)(2,1)S(1)} %all_gather.9, bf16[6144,384]{1,0:T(8,128)(2,1)} %param.9), kind=kOutput, calls=%fused_computation.28 | convolution fusion | flops 1207959552 | bytes 11206656 | tf_op jit(solution)/shard_map/dot_general | solution.py:28
  17.0 0.0 all-reduce.2.cloned.1.call-update
  17.0 0.0 reduce-scatter.10.cloned.1.call-start
  17.0 0.0 copy-done
  17.0 1.9 all_gather.11
  19.0 41.8 %all-gather.2.cloned.1.call-done = bf16[256,6144]{1,0:T(8,128)(2,1)} async-done(((bf16[16,6144]{1,0:T(8,128)(2,1)}), bf16[256,6144]{1,0:T(8,128)(2,1)}) %all-gather.2.cloned.1.call-update) | async-done | bytes 3145744 | tf_op jit(solution)/shard_map/all_gather | solution.py:44
  60.8 124.6 %all-reduce.2.cloned.1.call-done = f32[256,6144]{1,0:T(8,128)} async-done(((f32[256,6144]{1,0:T(8,128)}), f32[256,6144]{1,0:T(8,128)}) %all-reduce.2.cloned.1.call-update) | async-done | bytes 6291472 | tf_op jit(solution)/shard_map/psum | solution.py:46
  185.3 6.5 %fusion.6 = bf16[256,6144]{1,0:T(8,128)(2,1)S(1)} fusion(f32[256,6144]{1,0:T(8,128)} %all-reduce.2.cloned.1.call-done, bf16[256,6144]{1,0:T(8,128)(2,1)} %all-gather.2.cloned.1.call-done), kind=kLoop, calls=%fused_computation.15 | loop fusion | flops 31457280 | bytes 12582912 | tf_op jit(solution)/shard_map/convert_element_type | solution.py:47
  191.9 5.5 %multiply_bitcast_fusion = f32[384,6144]{0,1:T(8,128)} fusion(bf16[256,6144]{1,0:T(8,128)(2,1)S(1)} %fusion.6, bf16[256,384]{1,0:T(8,128)(2,1)S(1)} %all_gather.11), kind=kOutput, calls=%fused_computation.7 | convolution fusion | flops 1210318848 | bytes 12779520 | tf_op jit(solution)/shard_map/dot_general | solution.py:34
  197.4 9.7 %copy.10 = f32[384,6144]{1,0:T(8,128)} copy(f32[384,6144]{0,1:T(8,128)} %multiply_bitcast_fusion) | data formatting | bytes 18874368
  207.1 0.0 reduce-scatter.10.cloned.1.call-update
  207.1 0.0 reduce-scatter.6.cloned.1.call-start
  207.1 4.9 %fusion.21 = f32[256,384]{1,0:T(8,128)} fusion(bf16[256,6144]{1,0:T(8,128)(2,1)S(1)} %fusion.6, bf16[384,6144]{1,0:T(8,128)(2,1)} %param.8), kind=kOutput, calls=%fused_computation.29 | convolution fusion | flops 1207959552 | bytes 8257536 | tf_op jit(solution)/shard_map/dot_general | solution.py:28
  212.0 0.0 reduce-scatter.6.cloned.1.call-update
  212.1 0.0 reduce-scatter.8.cloned.1.call-start
  212.1 9.1 %convolution_multiply_fusion = f32[6144,384]{1,0:T(8,128)} fusion(bf16[256,384]{1,0:T(8,128)(2,1)S(1)} %all_gather.9, bf16[256,6144]{1,0:T(8,128)(2,1)} %all-gather.2.cloned.1.call-done), kind=kOutput, calls=%fused_computation.8 | convolution fusion | flops 1226047488 | bytes 12779520 | tf_op jit(solution)/shard_map/dot_general | solution.py:34
  221.2 0.0 reduce-scatter.8.cloned.1.call-update
  221.2 74.7 %reduce-scatter.10.cloned.1.call-done = f32[96,6144]{1,0:T(8,128)} async-done(((f32[384,6144]{1,0:T(8,128)}), f32[96,6144]{1,0:T(8,128)}) %reduce-scatter.10.cloned.1.call-update) | async-done | bytes 2359312
  295.9 2.2 copy.11
  298.1 2.2 copy.9
  300.3 8.6 %reduce-scatter.6.cloned.1.call-done = f32[128,384]{1,0:T(8,128)} async-done(((f32[256,384]{1,0:T(8,128)}), f32[128,384]{1,0:T(8,128)}) %reduce-scatter.6.cloned.1.call-update) | async-done | bytes 196624 | tf_op jit(solution)/shard_map/reduce_scatter | solution.py:49
  308.9 93.4 %reduce-scatter.8.cloned.1.call-done = f32[1536,384]{1,0:T(8,128)} async-done(((f32[6144,384]{1,0:T(8,128)}), f32[1536,384]{1,0:T(8,128)}) %reduce-scatter.8.cloned.1.call-update) | async-done | bytes 2359312 | tf_op jit(solution)/shard_map/reduce_scatter | solution.py:61
Async XLA Ops:
  7.2 53.6 %all-gather.2.cloned.1.call-start = ((), (), s32[]{:S(2)}) async-start(), calls=%async_computation.4 | async-start | bytes 3342336 | tf_op jit(solution)/shard_map/all_gather | solution.py:44
  7.9 177.4 %all-reduce.2.cloned.1.call-start = ((), (), s32[]{:S(2)}) async-start(), calls=%async_computation.3 | async-start | bytes 12582912 | tf_op jit(solution)/shard_map/psum | solution.py:46
  10.1 6.9 %copy-start = (bf16[128,384]{1,0:T(8,128)(2,1)S(1)}, bf16[128,384]{1,0:T(8,128)(2,1)}, u32[]{:S(2)}) copy-start(bf16[128,384]{1,0:T(8,128)(2,1)} %param.5) | copy-start | bytes 294916
  17.0 278.9 %reduce-scatter.10.cloned.1.call-start = ((), (), s32[]{:S(2)}) async-start(), calls=%async_computation.7 | async-start | bytes 11796480
  207.1 101.8 %reduce-scatter.6.cloned.1.call-start = ((), (), s32[]{:S(2)}) async-start(), calls=%async_computation.5 | async-start | bytes 589824 | tf_op jit(solution)/shard_map/reduce_scatter | solution.py:49
  212.1 190.2 %reduce-scatter.8.cloned.1.call-start = ((), (), s32[]{:S(2)}) async-start(), calls=%async_computation.6 | async-start | bytes 11796480 | tf_op jit(solution)/shard_map/reduce_scatter | solution.py:61
Sparse Core Ops, SparseCore 0:
  10.1 50.5 all-gather.1
  64.2 121.1 all-reduce.1
  207.2 88.6 reduce-scatter.9
  298.8 10.0 reduce-scatter.5
  311.7 90.4 reduce-scatter.7
where the time goes:
time: 410 us; the launch traced here: 409 us
  waiting for transfers between devices  344 us (84%)
  matrix products  26.3 us (6%)
  local copies, waits for them, and re-layouts  14.1 us (3%)
  between operations  13.8 us (3%)
  other arithmetic  6.55 us (2%)
  blocking collectives  4.11 us (1%)
    psum x1, waiting for transfers between devices, on_device(): grad_act = lax.psum(partial_act, 'row')  125 us
    reduce_scatter x1, waiting for transfers between devices, on_device(): lax.psum_scatter(transposed_times(hidden_all, cot_all) * norm_factor, 'de...  93.4 us
    unnamed x6, waiting for transfers between devices  75.4 us
    all_gather x1, waiting for transfers between devices, on_device(): lax.all_gather(pre_act, 'row', axis=0, tiled=True).astype(jnp.float32)  41.8 us
    dot_general x2, matrix products, transposed_times(): lax.dot_general(left, right, (((0,), (0,)), ((), ())), preferred_element_...  14.5 us
    unnamed x5, local copies, waits for them, and re-layouts  14.1 us
    dot_general x2, matrix products, times_transposed(): lax.dot_general(left, right, (((1,), (1,)), ((), ())), preferred_element_...  11.7 us
    reduce_scatter x1, waiting for transfers between devices, on_device(): lax.psum_scatter(times_transposed(grad_pre_all, w_in), 'col', scatter_dim...  8.55 us
  transfers between devices with their start and end apart: 5, of which 5 were waited for; matrix products, arithmetic and copies ran while one was open for 6% of the time, Pallas kernels for 0%

commit v1 on v0

v1 whole, which is shorter than its diff:
```python
import functools
import math

import jax
import jax.numpy as jnp
from jax import lax
from jax.experimental import pallas as pl
from jax.experimental.pallas import tpu as pltpu
from jax.sharding import PartitionSpec as P

MESH = pl.DeviceIdType.MESH
F32, BF16 = jnp.float32, jnp.bfloat16
RING = 4
WIDTHS = (1024, 1024, 1024, 1024, 1024, 1024)
ORDER = (
    2, 2, 3, 3, 4, 4, 5, 5, 8, 2, 0, 3, 0, 8, 5, 4, 2, 1, 3, 1, 5, 0, 4, 7, 1, 6, 3, 2, 5, 0, 1, 4,
    6, 3, 2, 5, 7, 0, 4, 1, 3, 2, 0, 5, 1, 8, 2, 4, 3, 0, 5, 2, 1, 4, 3, 3, 0, 5, 1, 6, 7, 5, 0, 2,
    1, 4, 1, 0, 4, 6, 7, 3, 9, 4, 1, 2, 0, 6, 5, 6, 7, 7, 9,
)
TILE = 768

gelu_coef = 0.044715
root = math.sqrt(2.0 / math.pi)


def gelu_and_slope(v):
    tanh_u = jnp.tanh(root * (v + gelu_coef * v * v * v))
    gelu = 0.5 * v * (1.0 + tanh_u)
    slope = 0.5 * (1.0 + tanh_u) + 0.5 * v * (1.0 - tanh_u * tanh_u) * root * (
        1.0 + 3.0 * gelu_coef * v * v
    )
    return gelu, slope


def nt(left, right):
    return lax.dot_general(
        left, right, (((1,), (1,)), ((), ())), preferred_element_type=F32
    )


def nn(left, right):
    return lax.dot_general(
        left, right, (((1,), (0,)), ((), ())), preferred_element_type=F32
    )


SHIFT = 2.0**20


def coded(v):
    v = v * jnp.abs(v)
    return (v * jnp.abs(v)).astype(BF16)


def decoded(t):
    t = t.astype(F32)
    r = lax.rsqrt(jnp.maximum(jnp.abs(t), 1e-37))
    return (t * r) * (r * lax.rsqrt(r))


def tn(left, right):
    return lax.dot_general(
        left, right, (((0,), (0,)), ((), ())), preferred_element_type=F32
    )


class Copies:
    def __init__(self, send_sems, recv_sems):
        self.send_sems, self.recv_sems = send_sems, recv_sems
        self.all, self.settled = [], 0

    def send(self, src, dst, to):
        n = len(self.all)
        copy = pltpu.make_async_remote_copy(
            src_ref=src,
            dst_ref=dst,
            send_sem=self.send_sems.at[n],
            recv_sem=self.recv_sems.at[n],
            device_id=to,
            device_id_type=MESH,
        )
        copy.start()
        self.all.append(copy)
        return copy


def kernel(
    n_copies, norm_factor, acts, cot, pre, w_in, w_out,
    gi_out, gwi_out, gwo_out,
    hid_full, acts_in, pre_v, w_in_v, w_out_v, cot_v, cot_scaled, cot_full, gwi_recv, gi, gi_recv, gi_sum, gi_depth,
    acts_v, acts_x, acts_all, slope_v, hid_v,
    part, part16, relay1, final1, mid, mid16, final2, gp, gq, xpart,
    send_sems, recv_sems, local_sems,
):
    x, row, c = lax.axis_index("depth"), lax.axis_index("row"), lax.axis_index("col")
    z, y = row // RING, row % RING
    feats, hid_size = w_in.shape
    toks, rows = acts.shape[0], feats // RING
    starts = [sum(WIDTHS[:k]) for k in range(len(WIDTHS))]

    def turn(i, step):
        return lax.rem(i + (step + RING), RING)

    def at(axis, step):
        if axis == "x":
            return (turn(x, step), row, c)
        if axis == "z":
            return (x, turn(z, step) * RING + y, c)
        return (x, z * RING + turn(y, step), c)

    place = {"x": x, "y": y, "z": z}
    other_core = (x, row, 1 - c)

    quarter = hid_size // RING

    def quarter_of(i):
        return pl.ds(pl.multiple_of(i * quarter, quarter), quarter)

    w_out_copies = [
        pltpu.make_async_copy(
            w_out.at[:, pl.ds(start // RING, width // RING)],
            w_out_v.at[:, pl.ds(start // RING, width // RING)],
            local_sems.at[k],
        )
        for k, (start, width) in enumerate(zip(starts, WIDTHS))
    ]
    w_in_copy = pltpu.make_async_copy(w_in.at[:, quarter_of(x)], w_in_v, local_sems.at[len(WIDTHS)])
    cot_copy = pltpu.make_async_copy(cot, cot_v.at[c], local_sems.at[len(WIDTHS) + 1])
    acts_copy = pltpu.make_async_copy(acts, acts_in, local_sems.at[len(WIDTHS) + 2])
    pre_copy = pltpu.make_async_copy(pre, pre_v, local_sems.at[len(WIDTHS) + 3])
    for copy in (cot_copy, acts_copy, pre_copy):
        copy.start()

    partners = [at("x", 1), at("x", 2), at("x", 3), other_core]
    partners += [(turn(x, s), row, 1 - c) for s in (1, 2, 3)]
    partners += [at(axis, s) for axis in "zy" for s in (1, 2, 3)]
    barrier = pltpu.get_barrier_semaphore()
    for who in partners:
        pl.semaphore_signal(barrier, inc=1, device_id=who, device_id_type=MESH)

    for copy in w_out_copies:
        copy.start()

    acts_copy.wait()
    turned = acts_in[...].astype(F32).T.astype(BF16)
    lanes = pl.ds(pl.multiple_of(c * toks, toks), toks)
    for j in range(RING):
        acts_v[turn(j - x, RING), :, lanes] = turned[j * rows:(j + 1) * rows]
    cot_copy.wait()
    pl.semaphore_wait(barrier, len(partners))

    copies = Copies(send_sems, recv_sems)
    send = copies.send
    cot_core = send(cot_v.at[c], cot_v.at[c], other_core)
    w_in_copy.start()

    pre_copy.wait()

    @pl.loop(0, hid_size // TILE)
    def _(n):
        cols = pl.ds(pl.multiple_of(n * TILE, TILE), TILE)
        gelu, slope = gelu_and_slope(pre_v[:, cols].astype(F32))
        hid_v[:, cols] = gelu.astype(BF16)
        slope_v[:, cols] = slope * (1.0 / SHIFT)

    cot_core.wait_recv()
    cot_scaled[...] = cot_v[...] * jnp.array(SHIFT, BF16)
    early = {}

    def side():
        early["hid"] = [
            send(hid_v.at[:, quarter_of(turn(x, s))], hid_full.at[x, z, y], at("x", s))
            for s in (1, 3, 2)
        ]
        early["acts"] = send(acts_v.at[:, :, lanes], acts_v.at[:, :, lanes], other_core)
        hid_full[x, z, y] = hid_v[:, quarter_of(x)]
        yield
        early["acts_x"] = []
        for s in (1, 3, 2):
            for where in (at("x", s), (turn(x, s), row, 1 - c)):
                mine = acts_v.at[:, :, lanes]
                early["acts_x"].append(send(mine, acts_x.at[s - 1, :, :, lanes], where))
        yield
        early["cot"] = []
        for s in (1, 3, 2):
            for where in (at("x", s), (turn(x, s), row, 1 - c)):
                early["cot"].append(send(cot_v.at[c], cot_full.at[x, c], where))
        cot_full[x] = cot_v[...]

    def settle(keep):
        while len(copies.all) - copies.settled > keep:
            copies.all[copies.settled].wait_send()
            copies.settled += 1

    def gather(axis, source):
        i = place[axis]
        up, down = at(axis, 1), at(axis, 3)
        low, high = pl.ds(0, RING // 2), pl.ds(RING // 2, RING // 2)

        def push(i, depths, where):
            what = source(i).at[depths]
            return send(what, what, where)

        ups, downs = push(i, low, up), push(i, high, down)
        rest = [push(i, high, up), push(i, low, down)]
        yield
        ups.wait_recv()
        downs.wait_recv()
        rest.append(push(turn(i, 3), low, up))
        rest.append(push(turn(i, 1), high, down))
        yield
        for copy in rest:
            copy.wait_recv()

    def once(name, wait):
        if name not in early:
            early[name] = True
            wait()

    done = []

    def all_acts():
        early["acts"].wait_recv()
        for copy in early["acts_x"]:
            copy.wait_recv()
        acts_all[:, :, :2 * toks] = acts_v[...]
        for s in range(1, RING):
            there = slice(s * 2 * toks, (s + 1) * 2 * toks)
            acts_all[:RING - s, :, there] = acts_x[s - 1, s:]
            acts_all[RING - s:, :, there] = acts_x[s - 1, :s]

    def add_grad_in(start, width):
        once("w_in", w_in_copy.wait)
        cols = pl.ds(start, width)
        total = nt(gq[:, :, :, :, cols].reshape(-1, width), w_in_v[:, cols])
        total = total.reshape(gi.shape)
        early["summed"] = early.get("summed", 0) + width
        gi[...] = total if early["summed"] == width else gi[...] + total
        if early["summed"] == quarter:
            early["gi"] = send(gi.at[:, 1 - c], gi_recv, other_core)

    def grad_in_sum():
        early["gi"].wait_recv()
        gi_out[...] = gi[0, c] + gi_recv[0]
        gi_sum[...] = (gi[1:, c] + gi_recv[1:]).astype(BF16)
        finals = [send(gi_sum.at[s - 1], gi_depth.at[s - 1], at("x", -s)) for s in (2, 1, 3)]
        yield
        for copy in finals:
            copy.wait_recv()
        for s in range(RING - 1):
            gi_out[...] += gi_depth[s].astype(F32)

    def chunk(k):
        first, second = ("z", "y") if k % 2 == 0 else ("y", "z")
        a, b = place[first], place[second]
        start, width = starts[k], WIDTHS[k]
        half, size, q_start = width // 2, width // RING, start // RING
        cols, low, high = pl.ds(start, width), pl.ds(start, half), pl.ds(start + half, half)
        halves, q_cols = pl.ds(start // 2, half), pl.ds(q_start, size)

        def block(ref, i):
            return ref.at[i] if first == "z" else ref.at[:, i]

        def part_of(i):
            return pl.ds(pl.multiple_of(i * quarter + q_start, 128), size)

        w_out_copies[k].wait()
        weights = w_out_v[:, q_cols, :].reshape(width, feats)
        total = nt(cot_scaled[...].reshape(2 * toks, feats), weights)
        total = total.reshape(RING, RING, -1, width)
        part[:, :, :, cols] = total
        part16[:, :, :, cols] = coded(total)
        yield

        up, down = at(first, 1), at(first, 3)
        across, ahead, behind = turn(a, 2), turn(a, 1), turn(a, 3)
        relays = [
            send(block(part16, across).at[..., low], relay1.at[0, :, :, halves], up),
            send(block(part16, across).at[..., high], relay1.at[1, :, :, halves], down),
        ]
        finals = [
            send(block(part16, ahead).at[..., high], final1.at[0, :, :, high], up),
            send(block(part16, behind).at[..., low], final1.at[1, :, :, low], down),
        ]
        yield
        for n, (part_cols, i, where) in enumerate(((low, ahead, up), (high, behind, down))):
            relays[n].wait_recv()
            mine = block(part16, i).at[..., part_cols]
            mine[...] = coded(
                block(part, i)[..., part_cols] + decoded(relay1[n, :, :, halves])
            )
            finals.append(send(mine, final1.at[n, :, :, part_cols], where))
        yield
        for copy in finals:
            copy.wait_recv()
        total = block(part, a)[..., cols]
        total += decoded(final1[0, :, :, cols]) + decoded(final1[1, :, :, cols])
        mid[:, :, cols] = total
        mid16[:, :, cols] = coded(total)

        finals = [
            send(mid16.at[turn(b, s), :, cols], final2.at[s - 1, :, cols], at(second, s))
            for s in (2, 1, 3)
        ]
        yield
        for copy in finals:
            copy.wait_recv()
        grad_act = mid[b, :, cols]
        for n in range(RING - 1):
            grad_act += decoded(final2[n, :, cols])
        slope = jnp.concatenate(
            [slope_v[:, pl.ds(i * quarter + q_start, size)] for i in range(RING)], axis=1
        )
        gp[:, cols] = (grad_act * slope).astype(BF16)

        def mine_of(i):
            return pl.ds(pl.multiple_of(start + i * size, 128), size)

        swap = [
            send(gp.at[:, mine_of(turn(x, s))], gq.at[s, z, y, :, q_cols], at("x", s))
            for s in (2, 1, 3)
        ]
        gq[0, z, y, :, q_cols] = gp[:, mine_of(x)]
        yield
        for copy in swap:
            copy.wait_recv()

        mine = gq.at[:, z, y, :, q_cols]
        finals = [send(mine, mine, at(second, s)) for s in (2, 1, 3)]
        yield
        for copy in finals:
            copy.wait_recv()

        def rows_of(i):
            return (gq.at[:, i] if first == "z" else gq.at[:, :, i]).at[..., q_cols]

        yield from gather(first, rows_of)

        once("acts_all", all_acts)
        total = nn(
            acts_all[...].reshape(feats, -1), gq[:, :, :, :, q_cols].reshape(-1, size)
        )
        gwi_out[:, part_of(x)] = total[:rows] * norm_factor
        finals = []
        for j in (2, 1, 3):
            xpart[j - 1, :, q_cols] = total[j * rows:(j + 1) * rows].astype(BF16)
            finals.append(
                send(xpart.at[j - 1, :, q_cols], gwi_recv.at[:, part_of(x)], at("x", j))
            )
        yield
        if (k ^ 1) in done:
            add_grad_in(starts[k & ~1] // RING, (WIDTHS[k ^ 1] + width) // RING)
        done.append(k)
        yield
        settle(30)
        for copy in finals:
            copy.wait_recv()
        for j in range(1, RING):
            there = part_of(turn(x, j))
            gwi_out[:, there] = gwi_recv[:, there].astype(F32) * norm_factor

    def hidden(n):
        first, second = ("y", "z") if n == 0 else ("z", "y")
        size = quarter // 2
        mine = pl.ds(n * size, size)

        def line(i):
            return (hid_full.at[:, i, y] if first == "z" else hid_full.at[:, z, i]).at[..., mine]

        def plane(i):
            return (hid_full.at[:, i] if second == "z" else hid_full.at[:, :, i]).at[..., mine]

        def arrived(name):
            for copy in early[name]:
                copy.wait_recv()

        once("hid_there", functools.partial(arrived, "hid"))
        yield from gather(first, line)
        yield from gather(second, plane)
        yield
        once("cot_there", functools.partial(arrived, "cot"))
        total = tn(
            hid_full[:, :, :, :, mine].reshape(-1, size), cot_full[...].reshape(-1, feats)
        )
        gwo_out[mine, :] = total * norm_factor

    work = [chunk(k) for k in range(len(WIDTHS))] + [hidden(n) for n in range(2)] + [side(), grad_in_sum()]
    for i in ORDER:
        next(work[i], None)
    assert all(next(left, "done") == "done" for left in work)

    settle(0)
    assert len(copies.all) == n_copies, len(copies.all)


def store(*refs):
    sems = refs[-1]
    copies = [pltpu.make_async_copy(refs[i], refs[3 + i], sems.at[i]) for i in range(3)]
    for copy in copies:
        copy.start()
    for copy in copies:
        copy.wait()


def on_device(acts, cotangent, pre_act, w_in, w_out):
    hid, feats = w_out.shape
    toks, few = acts.shape[0], pre_act.shape[0]
    rows = feats // RING
    quarter = hid // RING
    quarters = (RING, RING, RING, few, quarter)
    n_copies = 24 * len(WIDTHS) + 45
    any_, vmem = pl.BlockSpec(memory_space=pl.ANY), pl.BlockSpec(memory_space=pltpu.VMEM)
    plane = (RING, few, hid)
    whole = (RING, RING, few, hid)
    norm_factor = 1.0 / math.sqrt(2 * toks * lax.axis_size("depth"))
    grad_in, grad_w_in, grad_w_out = pl.pallas_call(
        functools.partial(kernel, n_copies, norm_factor),
        out_shape=[
            pltpu.VMEM((toks, feats), F32),
            pltpu.VMEM((rows, hid), F32),
            pltpu.VMEM((hid // RING, feats), F32),
        ],
        in_specs=[any_] * 5,
        out_specs=[vmem] * 3,
        scratch_shapes=[
            pltpu.VMEM(quarters, BF16),
            pltpu.VMEM((toks, feats), BF16),
            pltpu.VMEM((few, hid), BF16),
            pltpu.VMEM((feats, quarter), BF16),
            pltpu.VMEM((RING, quarter, feats), BF16),
            pltpu.VMEM((2, toks, feats), BF16),
            pltpu.VMEM((2, toks, feats), BF16),
            pltpu.VMEM((RING, 2, toks, feats), BF16),
            pltpu.VMEM((rows, hid), BF16),
            pltpu.VMEM((RING, 2, toks, feats), F32),
            pltpu.VMEM((RING, toks, feats), F32),
            pltpu.VMEM((RING - 1, toks, feats), BF16),
            pltpu.VMEM((RING - 1, toks, feats), BF16),
            pltpu.VMEM((RING, rows, 2 * toks), BF16),
            pltpu.VMEM((RING - 1, RING, rows, 2 * toks), BF16),
            pltpu.VMEM((RING, rows, RING * 2 * toks), BF16),
            pltpu.VMEM((few, hid), F32),
            pltpu.VMEM((few, hid), BF16),
            pltpu.VMEM(whole, F32),
            pltpu.VMEM(whole, BF16),
            pltpu.VMEM((2, RING, few, hid // 2), BF16),
            pltpu.VMEM((2,) + plane, BF16),
            pltpu.VMEM(plane, F32),
            pltpu.VMEM(plane, BF16),
            pltpu.VMEM((RING - 1, few, hid), BF16),
            pltpu.VMEM((few, hid), BF16),
            pltpu.VMEM(quarters, BF16),
            pltpu.VMEM((RING - 1, rows, quarter), BF16),
            pltpu.SemaphoreType.DMA((n_copies,)),
            pltpu.SemaphoreType.DMA((n_copies,)),
            pltpu.SemaphoreType.DMA((len(WIDTHS) + 4,)),
        ],
        compiler_params=pltpu.CompilerParams(
            collective_id=0, has_side_effects=True, vmem_limit_bytes=52 * 2**20
        ),
        cost_estimate=pl.CostEstimate(
            flops=6 * 2 * toks * feats * hid, bytes_accessed=20 * 2**20, transcendentals=few * hid
        ),
        name="backward",
    )(acts, cotangent, pre_act, w_in, w_out.reshape(RING, quarter, feats))
    outs = (grad_in, grad_w_in, grad_w_out)
    grad_in, grad_w_in, grad_w_out = pl.pallas_call(
        store,
        out_shape=[jax.ShapeDtypeStruct(out.shape, F32) for out in outs],
        in_specs=[vmem] * 3,
        out_specs=[any_] * 3,
        scratch_shapes=[pltpu.SemaphoreType.DMA((3,))],
        compiler_params=pltpu.CompilerParams(vmem_limit_bytes=4 * 2**20),
        name="store",
    )(*[pltpu.with_memory_space_constraint(out, pltpu.VMEM) for out in outs])
    return grad_in, grad_w_in[None, None], grad_w_out[None, None]


def solution(mesh):
    in_specs = (
        P(("depth", "col"), "row"),
        P(("depth", "col"), "row"),
        P(("depth", "row"), "col"),
        P("row", "col"),
        P("col", "row"),
    )
    out_specs = (
        P(("depth", "col"), "row"),
        P("row", "depth", None, "col"),
        P("col", "depth", None, "row"),
    )
    return jax.shard_map(
        on_device, mesh=mesh, in_specs=in_specs, out_specs=out_specs, check_vma=False
    )
```

time: 410 us -> 72.4 us (0.18)
  waiting for transfers between devices: 344 us -> 0 us
  Pallas kernels: 0 us -> 71.1 us
  matrix products: 26.3 us -> 0 us
  local copies, waits for them, and re-layouts: 14.1 us -> 0 us
  between operations: 13.8 us -> 0.64 us
  other arithmetic: 6.55 us -> 0 us
  blocking collectives: 4.11 us -> 0 us
    psum x1 -> x0, waiting for transfers between devices: 125 us -> none  [on_device(): grad_act = lax.psum(partial_act, 'row')]
    reduce_scatter x2 -> x0, waiting for transfers between devices: 102 us -> none  [the longest x1 93.4 us: on_device(): lax.psum_scatter(transposed_times(hidden_all, cot_all) * norm_factor, 'de...]
    unnamed x6 -> x0, waiting for transfers between devices: 75.4 us -> none
    pallas_call x0 -> x2, Pallas kernels: none -> 71.1 us  [the longest x1 68.8 us: on_device(): pl.pallas_call(functools.partial(kernel, n_copies, norm_factor), out_shap...]
    all_gather x1 -> x0, waiting for transfers between devices: 41.8 us -> none  [on_device(): lax.all_gather(pre_act, 'row', axis=0, tiled=True).astype(jnp.float32)]
    dot_general x4 -> x0, matrix products: 26.3 us -> none  [the longest x2 14.5 us: transposed_times(): lax.dot_general(left, right, (((0,), (0,)), ((), ())), preferred_element_...]
    unnamed x5 -> x0, local copies, waits for them, and re-layouts: 14.1 us -> none
    convert_element_type x1 -> x0, other arithmetic: 6.55 us -> none  [on_device(): grad_pre_all = (grad_act * gelu_slope(pre_all)).astype(jnp.bfloat16)]
  transfers between devices with their start and end apart: 5 -> 0, of which waited for: 5 -> 0; matrix products, arithmetic and copies ran while one was open for 6% -> 0% of each run, Pallas kernels for 0% -> 0%
where the time goes in v1:
time: 72.4 us; the launch traced here: 71.7 us
  Pallas kernels  71.1 us (98%)
    pallas_call x1, Pallas kernels, on_device(): pl.pallas_call(functools.partial(kernel, n_copies, norm_factor), out_shap...  68.8 us
    pallas_call x1, Pallas kernels, on_device(): pl.pallas_call(store, out_shape=[jax.ShapeDtypeStruct(out.shape, F32) for...  2.27 us

profile of v1, /device:TPU:0, one launch (start us, length us, event | category | flops | bytes accessed | tf_op | source)
XLA Modules:
  0.0 71.7 jit_solution(1752583585036884863)
XLA Ops:
  0.6 68.8 %backward.1 = (f32[128,384]{1,0:T(8,128)S(1)}, f32[96,6144]{1,0:T(8,128)S(1)}, f32[1536,384]{1,0:T(8,128)S(1)}) custom-call(bf16[128,384]{1,0:T(8,128)(2,1)} %acts.1, bf16[128,384]{1,0:T(8,128)(2,1)} %cot.1, bf16[16,6144]{1,0:T(8,128)(2,1)} %pre.1, bf16[384,6144]{1,0:T(8,128)(2,1)} %w_in.1, bf16[4,1536,384]{2,1,0:T(8,128)(2,1)} %bitcast.3), custom_call_target="tpu_custom_call" | custom-call | flops 3623878656 | bytes 20971520 | tf_op jit(solution)/shard_map/backward/pallas_call | solution.py:416
  69.4 2.3 %store.1 = (f32[128,384]{1,0:T(8,128)}, f32[96,6144]{1,0:T(8,128)}, f32[1536,384]{1,0:T(8,128)}) custom-call(f32[128,384]{1,0:T(8,128)S(1)} %get-tuple-element.9.refs_0_, f32[96,6144]{1,0:T(8,128)S(1)} %get-tuple-element.10.refs_1_, f32[1536,384]{1,0:T(8,128)S(1)} %get-tuple-element.11.refs_2_), custom_call_target="tpu_custom_call" | custom-call | tf_op jit(solution)/shard_map/store/pallas_call | solution.py:467

commit v2 on v1

--- a/solution.py
+++ b/solution.py
@@ -12,10 +12,11 @@
 F32, BF16 = jnp.float32, jnp.bfloat16
 RING = 4
 WIDTHS = (1024, 1024, 1024, 1024, 1024, 1024)
+PIECES = (768, 768)
 ORDER = (
-    2, 2, 3, 3, 4, 4, 5, 5, 8, 2, 0, 3, 0, 8, 5, 4, 2, 1, 3, 1, 5, 0, 4, 7, 1, 6, 3, 2, 5, 0, 1, 4,
-    6, 3, 2, 5, 7, 0, 4, 1, 3, 2, 0, 5, 1, 8, 2, 4, 3, 0, 5, 2, 1, 4, 3, 3, 0, 5, 1, 6, 7, 5, 0, 2,
-    1, 4, 1, 0, 4, 6, 7, 3, 9, 4, 1, 2, 0, 6, 5, 6, 7, 7, 9,
+    1, 1, 0, 0, 5, 2, 8, 5, 2, 4, 3, 0, 3, 4, 8, 2, 1, 3, 5, 0, 4, 1, 3, 2, 5, 4, 6, 7, 0, 1, 2, 3,
+    4, 7, 5, 0, 1, 6, 2, 3, 5, 4, 0, 1, 2, 8, 5, 4, 1, 2, 3, 5, 4, 0, 1, 3, 7, 6, 2, 4, 5, 0, 4, 3,
+    0, 1, 5, 3, 2, 6, 2, 7, 9, 5, 1, 7, 0, 4, 7, 6, 3, 6, 9,
 )
 TILE = 768
 
@@ -163,17 +164,17 @@
         hid_v[:, cols] = gelu.astype(BF16)
         slope_v[:, cols] = slope * (1.0 / SHIFT)
 
+    early = {}
+    early["hid"] = [
+        send(hid_v.at[:, quarter_of(turn(x, s))], hid_full.at[x, z, y], at("x", s))
+        for s in (2, 1, 3)
+    ]
+    hid_full[x, z, y] = hid_v[:, quarter_of(x)]
     cot_core.wait_recv()
     cot_scaled[...] = cot_v[...] * jnp.array(SHIFT, BF16)
-    early = {}
 
     def side():
-        early["hid"] = [
-            send(hid_v.at[:, quarter_of(turn(x, s))], hid_full.at[x, z, y], at("x", s))
-            for s in (1, 3, 2)
-        ]
         early["acts"] = send(acts_v.at[:, :, lanes], acts_v.at[:, :, lanes], other_core)
-        hid_full[x, z, y] = hid_v[:, quarter_of(x)]
         yield
         early["acts_x"] = []
         for s in (1, 3, 2):
@@ -360,9 +361,9 @@
             gwi_out[:, there] = gwi_recv[:, there].astype(F32) * norm_factor
 
     def hidden(n):
-        first, second = ("y", "z") if n == 0 else ("z", "y")
-        size = quarter // 2
-        mine = pl.ds(n * size, size)
+        first, second = ("y", "z") if n % 2 == 0 else ("z", "y")
+        size = PIECES[n]
+        mine = pl.ds(sum(PIECES[:n]), size)
 
         def line(i):
             return (hid_full.at[:, i, y] if first == "z" else hid_full.at[:, z, i]).at[..., mine]
@@ -384,7 +385,7 @@
         )
         gwo_out[mine, :] = total * norm_factor
 
-    work = [chunk(k) for k in range(len(WIDTHS))] + [hidden(n) for n in range(2)] + [side(), grad_in_sum()]
+    work = [chunk(k) for k in range(len(WIDTHS))] + [hidden(n) for n in range(len(PIECES))] + [side(), grad_in_sum()]
     for i in ORDER:
         next(work[i], None)
     assert all(next(left, "done") == "done" for left in work)
@@ -395,7 +396,13 @@
 
 def store(*refs):
     sems = refs[-1]
-    copies = [pltpu.make_async_copy(refs[i], refs[3 + i], sems.at[i]) for i in range(3)]
+    copies = []
+    for src, dst in zip(refs[:3], refs[3:6]):
+        rows = src.shape[0] // 4
+        for n in range(4):
+            piece = pl.ds(n * rows, rows)
+            sem = sems.at[len(copies)]
+            copies.append(pltpu.make_async_copy(src.at[piece], dst.at[piece], sem))
     for copy in copies:
         copy.start()
     for copy in copies:
@@ -408,7 +415,7 @@
     rows = feats // RING
     quarter = hid // RING
     quarters = (RING, RING, RING, few, quarter)
-    n_copies = 24 * len(WIDTHS) + 45
+    n_copies = 24 * len(WIDTHS) + 12 * len(PIECES) + 21
     any_, vmem = pl.BlockSpec(memory_space=pl.ANY), pl.BlockSpec(memory_space=pltpu.VMEM)
     plane = (RING, few, hid)
     whole = (RING, RING, few, hid)
@@ -469,7 +476,7 @@
         out_shape=[jax.ShapeDtypeStruct(out.shape, F32) for out in outs],
         in_specs=[vmem] * 3,
         out_specs=[any_] * 3,
-        scratch_shapes=[pltpu.SemaphoreType.DMA((3,))],
+        scratch_shapes=[pltpu.SemaphoreType.DMA((12,))],
         compiler_params=pltpu.CompilerParams(vmem_limit_bytes=4 * 2**20),
         name="store",
     )(*[pltpu.with_memory_space_constraint(out, pltpu.VMEM) for out in outs])

time: 72.4 us -> 71.5 us (0.988)
  no operation moved by 1% of the time
where the time goes in v2:
time: 71.5 us; the launch traced here: 71.4 us
  Pallas kernels  70.8 us (99%)
    pallas_call x1, Pallas kernels, on_device(): pl.pallas_call(functools.partial(kernel, n_copies, norm_factor), out_shap...  68.4 us
    pallas_call x1, Pallas kernels, on_device(): pl.pallas_call(store, out_shape=[jax.ShapeDtypeStruct(out.shape, F32) for...  2.34 us

profile of v2, /device:TPU:0, one launch (start us, length us, event | category | flops | bytes accessed | tf_op | source)
XLA Modules:
  0.0 71.4 jit_solution(6992868518398559948)
XLA Ops:
  0.6 68.4 %backward.1 = (f32[128,384]{1,0:T(8,128)S(1)}, f32[96,6144]{1,0:T(8,128)S(1)}, f32[1536,384]{1,0:T(8,128)S(1)}) custom-call(bf16[128,384]{1,0:T(8,128)(2,1)} %acts.1, bf16[128,384]{1,0:T(8,128)(2,1)} %cot.1, bf16[16,6144]{1,0:T(8,128)(2,1)} %pre.1, bf16[384,6144]{1,0:T(8,128)(2,1)} %w_in.1, bf16[4,1536,384]{2,1,0:T(8,128)(2,1)} %bitcast.3), custom_call_target="tpu_custom_call" | custom-call | flops 3623878656 | bytes 20971520 | tf_op jit(solution)/shard_map/backward/pallas_call | solution.py:423
  69.1 2.3 %store.1 = (f32[128,384]{1,0:T(8,128)}, f32[96,6144]{1,0:T(8,128)}, f32[1536,384]{1,0:T(8,128)}) custom-call(f32[128,384]{1,0:T(8,128)S(1)} %get-tuple-element.9.refs_0_, f32[96,6144]{1,0:T(8,128)S(1)} %get-tuple-element.10.refs_1_, f32[1536,384]{1,0:T(8,128)S(1)} %get-tuple-element.11.refs_2_), custom_call_target="tpu_custom_call" | custom-call | tf_op jit(solution)/shard_map/store/pallas_call | solution.py:474

commit v3 on v2

--- a/solution.py
+++ b/solution.py
@@ -14,9 +14,9 @@
 WIDTHS = (1024, 1024, 1024, 1024, 1024, 1024)
 PIECES = (768, 768)
 ORDER = (
-    1, 1, 0, 0, 5, 2, 8, 5, 2, 4, 3, 0, 3, 4, 8, 2, 1, 3, 5, 0, 4, 1, 3, 2, 5, 4, 6, 7, 0, 1, 2, 3,
-    4, 7, 5, 0, 1, 6, 2, 3, 5, 4, 0, 1, 2, 8, 5, 4, 1, 2, 3, 5, 4, 0, 1, 3, 7, 6, 2, 4, 5, 0, 4, 3,
-    0, 1, 5, 3, 2, 6, 2, 7, 9, 5, 1, 7, 0, 4, 7, 6, 3, 6, 9,
+    2, 2, 5, 5, 3, 4, 4, 3, 2, 8, 8, 5, 4, 0, 3, 0, 1, 2, 5, 1, 3, 4, 0, 1, 7, 2, 5, 6, 0, 3, 1, 4,
+    2, 6, 5, 7, 3, 1, 0, 4, 2, 5, 8, 1, 0, 4, 2, 5, 3, 4, 1, 5, 3, 0, 2, 4, 1, 7, 0, 2, 4, 5, 6, 3,
+    3, 1, 1, 0, 0, 5, 2, 6, 3, 7, 9, 1, 0, 4, 7, 7, 6, 6, 9,
 )
 TILE = 768
 
@@ -230,10 +230,11 @@
             acts_all[:RING - s, :, there] = acts_x[s - 1, s:]
             acts_all[RING - s:, :, there] = acts_x[s - 1, :s]
 
-    def add_grad_in(start, width):
+    def add_grad_in(k):
         once("w_in", w_in_copy.wait)
-        cols = pl.ds(start, width)
-        total = nt(gq[:, :, :, :, cols].reshape(-1, width), w_in_v[:, cols])
+        width = (WIDTHS[k] + WIDTHS[k + 1]) // RING
+        pair = jnp.concatenate([gq[k], gq[k + 1]], axis=-1).reshape(-1, width)
+        total = nt(pair, w_in_v[:, pl.ds(starts[k] // RING, width)])
         total = total.reshape(gi.shape)
         early["summed"] = early.get("summed", 0) + width
         gi[...] = total if early["summed"] == width else gi[...] + total
@@ -255,12 +256,12 @@
         first, second = ("z", "y") if k % 2 == 0 else ("y", "z")
         a, b = place[first], place[second]
         start, width = starts[k], WIDTHS[k]
-        half, size, q_start = width // 2, width // RING, start // RING
-        cols, low, high = pl.ds(start, width), pl.ds(start, half), pl.ds(start + half, half)
-        halves, q_cols = pl.ds(start // 2, half), pl.ds(q_start, size)
-
-        def block(ref, i):
-            return ref.at[i] if first == "z" else ref.at[:, i]
+        size, q_start = width // RING, start // RING
+        cols, q_cols = pl.ds(start, width), pl.ds(q_start, size)
+        low, high = pl.ds(0, RING // 2), pl.ds(RING // 2, RING // 2)
+
+        def block(ref, i, half=slice(None)):
+            return ref.at[k, i, half] if first == "z" else ref.at[k, half, i]
 
         def part_of(i):
             return pl.ds(pl.multiple_of(i * quarter + q_start, 128), size)
@@ -269,96 +270,81 @@
         weights = w_out_v[:, q_cols, :].reshape(width, feats)
         total = nt(cot_scaled[...].reshape(2 * toks, feats), weights)
         total = total.reshape(RING, RING, -1, width)
-        part[:, :, :, cols] = total
-        part16[:, :, :, cols] = coded(total)
+        part[k] = total
+        part16[k] = coded(total)
         yield
 
         up, down = at(first, 1), at(first, 3)
         across, ahead, behind = turn(a, 2), turn(a, 1), turn(a, 3)
         relays = [
-            send(block(part16, across).at[..., low], relay1.at[0, :, :, halves], up),
-            send(block(part16, across).at[..., high], relay1.at[1, :, :, halves], down),
+            send(block(part16, across, low), relay1.at[k, 0], up),
+            send(block(part16, across, high), relay1.at[k, 1], down),
         ]
         finals = [
-            send(block(part16, ahead).at[..., high], final1.at[0, :, :, high], up),
-            send(block(part16, behind).at[..., low], final1.at[1, :, :, low], down),
+            send(block(part16, ahead, high), final1.at[k, 0, high], up),
+            send(block(part16, behind, low), final1.at[k, 1, low], down),
         ]
         yield
-        for n, (part_cols, i, where) in enumerate(((low, ahead, up), (high, behind, down))):
+        for n, (half, i, where) in enumerate(((low, ahead, up), (high, behind, down))):
             relays[n].wait_recv()
-            mine = block(part16, i).at[..., part_cols]
-            mine[...] = coded(
-                block(part, i)[..., part_cols] + decoded(relay1[n, :, :, halves])
-            )
-            finals.append(send(mine, final1.at[n, :, :, part_cols], where))
+            mine = block(part16, i, half)
+            mine[...] = coded(block(part, i, half)[...] + decoded(relay1[k, n]))
+            finals.append(send(mine, final1.at[k, n, half], where))
         yield
         for copy in finals:
             copy.wait_recv()
-        total = block(part, a)[..., cols]
-        total += decoded(final1[0, :, :, cols]) + decoded(final1[1, :, :, cols])
-        mid[:, :, cols] = total
-        mid16[:, :, cols] = coded(total)
+        total = block(part, a)[...] + decoded(final1[k, 0]) + decoded(final1[k, 1])
+        mid[k] = total
+        mid16[k] = coded(total)
 
         finals = [
-            send(mid16.at[turn(b, s), :, cols], final2.at[s - 1, :, cols], at(second, s))
-            for s in (2, 1, 3)
+            send(mid16.at[k, turn(b, s)], final2.at[k, s - 1], at(second, s)) for s in (2, 1, 3)
         ]
         yield
         for copy in finals:
             copy.wait_recv()
-        grad_act = mid[b, :, cols]
+        grad_act = mid[k, b]
         for n in range(RING - 1):
-            grad_act += decoded(final2[n, :, cols])
-        slope = jnp.concatenate(
-            [slope_v[:, pl.ds(i * quarter + q_start, size)] for i in range(RING)], axis=1
-        )
-        gp[:, cols] = (grad_act * slope).astype(BF16)
-
-        def mine_of(i):
-            return pl.ds(pl.multiple_of(start + i * size, 128), size)
-
-        swap = [
-            send(gp.at[:, mine_of(turn(x, s))], gq.at[s, z, y, :, q_cols], at("x", s))
-            for s in (2, 1, 3)
-        ]
-        gq[0, z, y, :, q_cols] = gp[:, mine_of(x)]
+            grad_act += decoded(final2[k, n])
+        for i in range(RING):
+            slope = slope_v[:, pl.ds(i * quarter + q_start, size)]
+            gp[k, i] = (grad_act[:, i * size:(i + 1) * size] * slope).astype(BF16)
+
+        swap = [send(gp.at[k, turn(x, s)], gq.at[k, s, z, y], at("x", s)) for s in (2, 1, 3)]
+        gq[k, 0, z, y] = gp[k, x]
         yield
         for copy in swap:
             copy.wait_recv()
 
-        mine = gq.at[:, z, y, :, q_cols]
+        mine = gq.at[k, :, z, y]
         finals = [send(mine, mine, at(second, s)) for s in (2, 1, 3)]
         yield
         for copy in finals:
             copy.wait_recv()
 
         def rows_of(i):
-            return (gq.at[:, i] if first == "z" else gq.at[:, :, i]).at[..., q_cols]
+            return gq.at[k, :, i] if first == "z" else gq.at[k, :, :, i]
 
         yield from gather(first, rows_of)
 
         once("acts_all", all_acts)
-        total = nn(
-            acts_all[...].reshape(feats, -1), gq[:, :, :, :, q_cols].reshape(-1, size)
-        )
+        total = nn(acts_all[...].reshape(feats, -1), gq[k].reshape(-1, size))
         gwi_out[:, part_of(x)] = total[:rows] * norm_factor
         finals = []
         for j in (2, 1, 3):
-            xpart[j - 1, :, q_cols] = total[j * rows:(j + 1) * rows].astype(BF16)
-            finals.append(
-                send(xpart.at[j - 1, :, q_cols], gwi_recv.at[:, part_of(x)], at("x", j))
-            )
+            xpart[k, j - 1] = total[j * rows:(j + 1) * rows].astype(BF16)
+            finals.append(send(xpart.at[k, j - 1], gwi_recv.at[k, j - 1], at("x", j)))
         yield
         if (k ^ 1) in done:
-            add_grad_in(starts[k & ~1] // RING, (WIDTHS[k ^ 1] + width) // RING)
+            add_grad_in(k & ~1)
         done.append(k)
         yield
         settle(30)
         for copy in finals:
             copy.wait_recv()
         for j in range(1, RING):
-            there = part_of(turn(x, j))
-            gwi_out[:, there] = gwi_recv[:, there].astype(F32) * norm_factor
+            there = part_of(turn(x, -j))
+            gwi_out[:, there] = gwi_recv[k, j - 1].astype(F32) * norm_factor
 
     def hidden(n):
         first, second = ("y", "z") if n % 2 == 0 else ("z", "y")
@@ -417,8 +403,9 @@
     quarters = (RING, RING, RING, few, quarter)
     n_copies = 24 * len(WIDTHS) + 12 * len(PIECES) + 21
     any_, vmem = pl.BlockSpec(memory_space=pl.ANY), pl.BlockSpec(memory_space=pltpu.VMEM)
-    plane = (RING, few, hid)
-    whole = (RING, RING, few, hid)
+    chunks, width = len(WIDTHS), WIDTHS[0]
+    size, plane = width // RING, (RING, few, width)
+    assert all(other == width for other in WIDTHS)
     norm_factor = 1.0 / math.sqrt(2 * toks * lax.axis_size("depth"))
     grad_in, grad_w_in, grad_w_out = pl.pallas_call(
         functools.partial(kernel, n_copies, norm_factor),
@@ -438,7 +425,7 @@
             pltpu.VMEM((2, toks, feats), BF16),
             pltpu.VMEM((2, toks, feats), BF16),
             pltpu.VMEM((RING, 2, toks, feats), BF16),
-            pltpu.VMEM((rows, hid), BF16),
+            pltpu.VMEM((chunks, RING - 1, rows, size), BF16),
             pltpu.VMEM((RING, 2, toks, feats), F32),
             pltpu.VMEM((RING, toks, feats), F32),
             pltpu.VMEM((RING - 1, toks, feats), BF16),
@@ -448,16 +435,16 @@
             pltpu.VMEM((RING, rows, RING * 2 * toks), BF16),
             pltpu.VMEM((few, hid), F32),
             pltpu.VMEM((few, hid), BF16),
-            pltpu.VMEM(whole, F32),
-            pltpu.VMEM(whole, BF16),
-            pltpu.VMEM((2, RING, few, hid // 2), BF16),
-            pltpu.VMEM((2,) + plane, BF16),
-            pltpu.VMEM(plane, F32),
-            pltpu.VMEM(plane, BF16),
-            pltpu.VMEM((RING - 1, few, hid), BF16),
-            pltpu.VMEM((few, hid), BF16),
-            pltpu.VMEM(quarters, BF16),
-            pltpu.VMEM((RING - 1, rows, quarter), BF16),
+            pltpu.VMEM((chunks, RING) + plane, F32),
+            pltpu.VMEM((chunks, RING) + plane, BF16),
+            pltpu.VMEM((chunks, 2, RING // 2) + plane[1:], BF16),
+            pltpu.VMEM((chunks, 2) + plane, BF16),
+            pltpu.VMEM((chunks,) + plane, F32),
+            pltpu.VMEM((chunks,) + plane, BF16),
+            pltpu.VMEM((chunks, RING - 1) + plane[1:], BF16),
+            pltpu.VMEM((chunks, RING, few, size), BF16),
+            pltpu.VMEM((chunks, RING, RING, RING, few, size), BF16),
+            pltpu.VMEM((chunks, RING - 1, rows, size), BF16),
             pltpu.SemaphoreType.DMA((n_copies,)),
             pltpu.SemaphoreType.DMA((n_copies,)),
             pltpu.SemaphoreType.DMA((len(WIDTHS) + 4,)),

time: 71.5 us -> 72.4 us (1.013)
  Pallas kernels: 70.8 us -> 71.6 us
    pallas_call x1, Pallas kernels: 68.4 us -> 69.3 us  [on_device(): pl.pallas_call(functools.partial(kernel, n_copies, norm_factor), out_shap...]
where the time goes in v3:
time: 72.4 us; the launch traced here: 72.2 us
  Pallas kernels  71.6 us (99%)
    pallas_call x1, Pallas kernels, on_device(): pl.pallas_call(functools.partial(kernel, n_copies, norm_factor), out_shap...  69.3 us
    pallas_call x1, Pallas kernels, on_device(): pl.pallas_call(store, out_shape=[jax.ShapeDtypeStruct(out.shape, F32) for...  2.34 us

profile of v3, /device:TPU:0, one launch (start us, length us, event | category | flops | bytes accessed | tf_op | source)
XLA Modules:
  0.0 72.2 jit_solution(3573568585314869484)
XLA Ops:
  0.6 69.3 %backward.1 = (f32[128,384]{1,0:T(8,128)S(1)}, f32[96,6144]{1,0:T(8,128)S(1)}, f32[1536,384]{1,0:T(8,128)S(1)}) custom-call(bf16[128,384]{1,0:T(8,128)(2,1)} %acts.1, bf16[128,384]{1,0:T(8,128)(2,1)} %cot.1, bf16[16,6144]{1,0:T(8,128)(2,1)} %pre.1, bf16[384,6144]{1,0:T(8,128)(2,1)} %w_in.1, bf16[4,1536,384]{2,1,0:T(8,128)(2,1)} %bitcast.3), custom_call_target="tpu_custom_call" | custom-call | flops 3623878656 | bytes 20971520 | tf_op jit(solution)/shard_map/backward/pallas_call | solution.py:410
  69.9 2.3 %store.1 = (f32[128,384]{1,0:T(8,128)}, f32[96,6144]{1,0:T(8,128)}, f32[1536,384]{1,0:T(8,128)}) custom-call(f32[128,384]{1,0:T(8,128)S(1)} %get-tuple-element.9.refs_0_, f32[96,6144]{1,0:T(8,128)S(1)} %get-tuple-element.10.refs_1_, f32[1536,384]{1,0:T(8,128)S(1)} %get-tuple-element.11.refs_2_), custom_call_target="tpu_custom_call" | custom-call | tf_op jit(solution)/shard_map/store/pallas_call | solution.py:461

commit v4 on v3

--- a/solution.py
+++ b/solution.py
@@ -14,9 +14,9 @@
 WIDTHS = (1024, 1024, 1024, 1024, 1024, 1024)
 PIECES = (768, 768)
 ORDER = (
-    2, 2, 5, 5, 3, 4, 4, 3, 2, 8, 8, 5, 4, 0, 3, 0, 1, 2, 5, 1, 3, 4, 0, 1, 7, 2, 5, 6, 0, 3, 1, 4,
-    2, 6, 5, 7, 3, 1, 0, 4, 2, 5, 8, 1, 0, 4, 2, 5, 3, 4, 1, 5, 3, 0, 2, 4, 1, 7, 0, 2, 4, 5, 6, 3,
-    3, 1, 1, 0, 0, 5, 2, 6, 3, 7, 9, 1, 0, 4, 7, 7, 6, 6, 9,
+    1, 1, 4, 4, 5, 0, 5, 3, 2, 2, 3, 0, 8, 8, 1, 4, 3, 0, 4, 1, 5, 3, 0, 2, 6, 4, 1, 5, 3, 7, 2, 0,
+    4, 1, 3, 5, 7, 6, 2, 0, 4, 1, 5, 8, 2, 0, 1, 4, 3, 0, 5, 2, 1, 3, 4, 5, 7, 2, 0, 0, 6, 3, 1, 5,
+    3, 4, 2, 2, 5, 7, 6, 4, 9, 7, 0, 3, 7, 6, 6, 9, 2, 5, 1,
 )
 TILE = 768
 
@@ -129,24 +129,16 @@
     cot_copy = pltpu.make_async_copy(cot, cot_v.at[c], local_sems.at[len(WIDTHS) + 1])
     acts_copy = pltpu.make_async_copy(acts, acts_in, local_sems.at[len(WIDTHS) + 2])
     pre_copy = pltpu.make_async_copy(pre, pre_v, local_sems.at[len(WIDTHS) + 3])
-    for copy in (cot_copy, acts_copy, pre_copy):
-        copy.start()
-
-    partners = [at("x", 1), at("x", 2), at("x", 3), other_core]
-    partners += [(turn(x, s), row, 1 - c) for s in (1, 2, 3)]
-    partners += [at(axis, s) for axis in "zy" for s in (1, 2, 3)]
+
+    partners = [other_core] + [at(axis, s) for axis in "zy" for s in (1, 2, 3)]
+    partners += [(turn(x, s), row, core) for core in (c, 1 - c) for s in (1, 2, 3)]
     barrier = pltpu.get_barrier_semaphore()
     for who in partners:
         pl.semaphore_signal(barrier, inc=1, device_id=who, device_id_type=MESH)
 
-    for copy in w_out_copies:
+    for copy in [cot_copy, pre_copy, *w_out_copies, acts_copy]:
         copy.start()
-
-    acts_copy.wait()
-    turned = acts_in[...].astype(F32).T.astype(BF16)
     lanes = pl.ds(pl.multiple_of(c * toks, toks), toks)
-    for j in range(RING):
-        acts_v[turn(j - x, RING), :, lanes] = turned[j * rows:(j + 1) * rows]
     cot_copy.wait()
     pl.semaphore_wait(barrier, len(partners))
 
@@ -174,6 +166,10 @@
     cot_scaled[...] = cot_v[...] * jnp.array(SHIFT, BF16)
 
     def side():
+        acts_copy.wait()
+        turned = acts_in[...].astype(F32).T.astype(BF16)
+        for j in range(RING):
+            acts_v[turn(j - x, RING), :, lanes] = turned[j * rows:(j + 1) * rows]
         early["acts"] = send(acts_v.at[:, :, lanes], acts_v.at[:, :, lanes], other_core)
         yield
         early["acts_x"] = []
@@ -280,16 +276,13 @@
             send(block(part16, across, low), relay1.at[k, 0], up),
             send(block(part16, across, high), relay1.at[k, 1], down),
         ]
-        finals = [
-            send(block(part16, ahead, high), final1.at[k, 0, high], up),
-            send(block(part16, behind, low), final1.at[k, 1, low], down),
-        ]
+        finals = []
         yield
         for n, (half, i, where) in enumerate(((low, ahead, up), (high, behind, down))):
             relays[n].wait_recv()
             mine = block(part16, i, half)
             mine[...] = coded(block(part, i, half)[...] + decoded(relay1[k, n]))
-            finals.append(send(mine, final1.at[k, n, half], where))
+            finals.append(send(block(part16, i), final1.at[k, n], where))
         yield
         for copy in finals:
             copy.wait_recv()
@@ -401,7 +394,7 @@
     rows = feats // RING
     quarter = hid // RING
     quarters = (RING, RING, RING, few, quarter)
-    n_copies = 24 * len(WIDTHS) + 12 * len(PIECES) + 21
+    n_copies = 22 * len(WIDTHS) + 12 * len(PIECES) + 21
     any_, vmem = pl.BlockSpec(memory_space=pl.ANY), pl.BlockSpec(memory_space=pltpu.VMEM)
     chunks, width = len(WIDTHS), WIDTHS[0]
     size, plane = width // RING, (RING, few, width)

time: 72.4 us -> 71 us (0.981)
  Pallas kernels: 71.6 us -> 70.3 us
    pallas_call x1, Pallas kernels: 69.3 us -> 67.9 us  [on_device(): pl.pallas_call(functools.partial(kernel, n_copies, norm_factor), out_shap...]
where the time goes in v4:
time: 71 us; the launch traced here: 70.9 us
  Pallas kernels  70.3 us (99%)
    pallas_call x1, Pallas kernels, on_device(): pl.pallas_call(functools.partial(kernel, n_copies, norm_factor), out_shap...  67.9 us
    pallas_call x1, Pallas kernels, on_device(): pl.pallas_call(store, out_shape=[jax.ShapeDtypeStruct(out.shape, F32) for...  2.34 us

profile of v4, /device:TPU:0, one launch (start us, length us, event | category | flops | bytes accessed | tf_op | source)
XLA Modules:
  0.0 70.9 jit_solution(8733908865020334724)
XLA Ops:
  0.6 67.9 %backward.1 = (f32[128,384]{1,0:T(8,128)S(1)}, f32[96,6144]{1,0:T(8,128)S(1)}, f32[1536,384]{1,0:T(8,128)S(1)}) custom-call(bf16[128,384]{1,0:T(8,128)(2,1)} %acts.1, bf16[128,384]{1,0:T(8,128)(2,1)} %cot.1, bf16[16,6144]{1,0:T(8,128)(2,1)} %pre.1, bf16[384,6144]{1,0:T(8,128)(2,1)} %w_in.1, bf16[4,1536,384]{2,1,0:T(8,128)(2,1)} %bitcast.3), custom_call_target="tpu_custom_call" | custom-call | flops 3623878656 | bytes 20971520 | tf_op jit(solution)/shard_map/backward/pallas_call | solution.py:403
  68.6 2.3 %store.1 = (f32[128,384]{1,0:T(8,128)}, f32[96,6144]{1,0:T(8,128)}, f32[1536,384]{1,0:T(8,128)}) custom-call(f32[128,384]{1,0:T(8,128)S(1)} %get-tuple-element.9.refs_0_, f32[96,6144]{1,0:T(8,128)S(1)} %get-tuple-element.10.refs_1_, f32[1536,384]{1,0:T(8,128)S(1)} %get-tuple-element.11.refs_2_), custom_call_target="tpu_custom_call" | custom-call | tf_op jit(solution)/shard_map/store/pallas_call | solution.py:454

commit v5 on v4

--- a/solution.py
+++ b/solution.py
@@ -365,7 +365,9 @@
         gwo_out[mine, :] = total * norm_factor
 
     work = [chunk(k) for k in range(len(WIDTHS))] + [hidden(n) for n in range(len(PIECES))] + [side(), grad_in_sum()]
-    for i in ORDER:
+    for n, i in enumerate(ORDER):
+        if n == len(ORDER) - 3:
+            settle(12)
         next(work[i], None)
     assert all(next(left, "done") == "done" for left in work)
 
@@ -375,13 +377,7 @@
 
 def store(*refs):
     sems = refs[-1]
-    copies = []
-    for src, dst in zip(refs[:3], refs[3:6]):
-        rows = src.shape[0] // 4
-        for n in range(4):
-            piece = pl.ds(n * rows, rows)
-            sem = sems.at[len(copies)]
-            copies.append(pltpu.make_async_copy(src.at[piece], dst.at[piece], sem))
+    copies = [pltpu.make_async_copy(refs[i], refs[3 + i], sems.at[i]) for i in range(3)]
     for copy in copies:
         copy.start()
     for copy in copies:
@@ -456,7 +452,7 @@
         out_shape=[jax.ShapeDtypeStruct(out.shape, F32) for out in outs],
         in_specs=[vmem] * 3,
         out_specs=[any_] * 3,
-        scratch_shapes=[pltpu.SemaphoreType.DMA((12,))],
+        scratch_shapes=[pltpu.SemaphoreType.DMA((3,))],
         compiler_params=pltpu.CompilerParams(vmem_limit_bytes=4 * 2**20),
         name="store",
     )(*[pltpu.with_memory_space_constraint(out, pltpu.VMEM) for out in outs])

time: 71 us -> 71 us (level)
  no operation moved by 1% of the time
where the time goes in v5:
time: 71 us; the launch traced here: 70.9 us
  Pallas kernels  70.2 us (99%)
    pallas_call x1, Pallas kernels, on_device(): pl.pallas_call(functools.partial(kernel, n_copies, norm_factor), out_shap...  67.9 us
    pallas_call x1, Pallas kernels, on_device(): pl.pallas_call(store, out_shape=[jax.ShapeDtypeStruct(out.shape, F32) for...  2.27 us

profile of v5, /device:TPU:0, one launch (start us, length us, event | category | flops | bytes accessed | tf_op | source)
XLA Modules:
  0.0 70.9 jit_solution(4176343514178523461)
XLA Ops:
  0.6 67.9 %backward.1 = (f32[128,384]{1,0:T(8,128)S(1)}, f32[96,6144]{1,0:T(8,128)S(1)}, f32[1536,384]{1,0:T(8,128)S(1)}) custom-call(bf16[128,384]{1,0:T(8,128)(2,1)} %acts.1, bf16[128,384]{1,0:T(8,128)(2,1)} %cot.1, bf16[16,6144]{1,0:T(8,128)(2,1)} %pre.1, bf16[384,6144]{1,0:T(8,128)(2,1)} %w_in.1, bf16[4,1536,384]{2,1,0:T(8,128)(2,1)} %bitcast.3), custom_call_target="tpu_custom_call" | custom-call | flops 3623878656 | bytes 20971520 | tf_op jit(solution)/shard_map/backward/pallas_call | solution.py:399
  68.6 2.3 %store.1 = (f32[128,384]{1,0:T(8,128)}, f32[96,6144]{1,0:T(8,128)}, f32[1536,384]{1,0:T(8,128)}) custom-call(f32[128,384]{1,0:T(8,128)S(1)} %get-tuple-element.9.refs_0_, f32[96,6144]{1,0:T(8,128)S(1)} %get-tuple-element.10.refs_1_, f32[1536,384]{1,0:T(8,128)S(1)} %get-tuple-element.11.refs_2_), custom_call_target="tpu_custom_call" | custom-call | tf_op jit(solution)/shard_map/store/pallas_call | solution.py:450

commit v6 on v5

--- a/solution.py
+++ b/solution.py
@@ -131,7 +131,7 @@
     pre_copy = pltpu.make_async_copy(pre, pre_v, local_sems.at[len(WIDTHS) + 3])
 
     partners = [other_core] + [at(axis, s) for axis in "zy" for s in (1, 2, 3)]
-    partners += [(turn(x, s), row, core) for core in (c, 1 - c) for s in (1, 2, 3)]
+    partners += [at("x", s) for s in (1, 2, 3)]
     barrier = pltpu.get_barrier_semaphore()
     for who in partners:
         pl.semaphore_signal(barrier, inc=1, device_id=who, device_id_type=MESH)
@@ -172,16 +172,19 @@
             acts_v[turn(j - x, RING), :, lanes] = turned[j * rows:(j + 1) * rows]
         early["acts"] = send(acts_v.at[:, :, lanes], acts_v.at[:, :, lanes], other_core)
         yield
-        early["acts_x"] = []
-        for s in (1, 3, 2):
-            for where in (at("x", s), (turn(x, s), row, 1 - c)):
-                mine = acts_v.at[:, :, lanes]
-                early["acts_x"].append(send(mine, acts_x.at[s - 1, :, :, lanes], where))
-        yield
-        early["cot"] = []
-        for s in (1, 3, 2):
-            for where in (at("x", s), (turn(x, s), row, 1 - c)):
-                early["cot"].append(send(cot_v.at[c], cot_full.at[x, c], where))
+        mine = acts_v.at[:, :, lanes]
+        early["acts_x"] = [send(mine, acts_x.at[s - 1, :, :, lanes], at("x", s)) for s in (1, 3, 2)]
+        early["cot"] = [send(cot_v.at[c], cot_full.at[x, c], at("x", s)) for s in (1, 3, 2)]
+        yield
+        for copy, s in zip(list(early["acts_x"]), (1, 3, 2)):
+            copy.wait_recv()
+            here = acts_x.at[s - 1, :, :, lanes]
+            early["acts_x"].append(send(here, here, other_core))
+        for copy, s in zip(list(early["cot"]), (1, 3, 2)):
+            copy.wait_recv()
+            here = cot_full.at[turn(x, -s), c]
+            early["cot"].append(send(here, here, other_core))
+        del early["acts_x"][:3], early["cot"][:3]
         cot_full[x] = cot_v[...]
 
     def settle(keep):

time: 71 us -> 72 us (1.014)
  Pallas kernels: 70.2 us -> 71.3 us
    pallas_call x1, Pallas kernels: 67.9 us -> 69 us  [on_device(): pl.pallas_call(functools.partial(kernel, n_copies, norm_factor), out_shap...]
where the time goes in v6:
time: 72 us; the launch traced here: 71.9 us
  Pallas kernels  71.3 us (99%)
    pallas_call x1, Pallas kernels, on_device(): pl.pallas_call(functools.partial(kernel, n_copies, norm_factor), out_shap...  69 us
    pallas_call x1, Pallas kernels, on_device(): pl.pallas_call(store, out_shape=[jax.ShapeDtypeStruct(out.shape, F32) for...  2.27 us

profile of v6, /device:TPU:0, one launch (start us, length us, event | category | flops | bytes accessed | tf_op | source)
XLA Modules:
  0.0 71.9 jit_solution(14793446484816049956)
XLA Ops:
  0.6 69.0 %backward.1 = (f32[128,384]{1,0:T(8,128)S(1)}, f32[96,6144]{1,0:T(8,128)S(1)}, f32[1536,384]{1,0:T(8,128)S(1)}) custom-call(bf16[128,384]{1,0:T(8,128)(2,1)} %acts.1, bf16[128,384]{1,0:T(8,128)(2,1)} %cot.1, bf16[16,6144]{1,0:T(8,128)(2,1)} %pre.1, bf16[384,6144]{1,0:T(8,128)(2,1)} %w_in.1, bf16[4,1536,384]{2,1,0:T(8,128)(2,1)} %bitcast.3), custom_call_target="tpu_custom_call" | custom-call | flops 3623878656 | bytes 20971520 | tf_op jit(solution)/shard_map/backward/pallas_call | solution.py:402
  69.6 2.3 %store.1 = (f32[128,384]{1,0:T(8,128)}, f32[96,6144]{1,0:T(8,128)}, f32[1536,384]{1,0:T(8,128)}) custom-call(f32[128,384]{1,0:T(8,128)S(1)} %get-tuple-element.9.refs_0_, f32[96,6144]{1,0:T(8,128)S(1)} %get-tuple-element.10.refs_1_, f32[1536,384]{1,0:T(8,128)S(1)} %get-tuple-element.11.refs_2_), custom_call_target="tpu_custom_call" | custom-call | tf_op jit(solution)/shard_map/store/pallas_call | solution.py:453
